TPU v7x, 32 devices: a whole 2x2x4 slice. The times are simulated.
32 devices in a mesh: shard: 8 (over y, x, core), ctx: 4 (over z).
Axes of the slice: x: 2, y: 2, z: 4, core: 2. Of those that a mesh axis runs over, the one named last changes fastest.
Arguments:
- tokens: bfloat16 [8, 1536, 768], P('shard', 'ctx'), may hold values from -6 to 6
- cotangent: bfloat16 [8, 1536, 768], P('shard', 'ctx'), may hold values from -6 to 6
- doc_lengths: int32 [8, 4], P('shard'), may hold values from 0 to 1536, as said below
- w_qkv: bfloat16 [768, 2304], P('shard'), may hold values from -0.21875 to 0.21875
- w_out: bfloat16 [768, 768], P('shard'), may hold values from -6 to 6
- w_in: bfloat16 [768, 3072], P('shard'), may hold values from -0.21875 to 0.21875
- w_down: bfloat16 [3072, 768], P('shard'), may hold values from -0.109375 to 0.109375
- bias_query: bfloat16 [768], P('shard'), may hold values from -1.5 to 1.5
- bias_value: bfloat16 [768], P('shard'), may hold values from -0.3125 to 0.3125
- bias_out: bfloat16 [768], P('shard'), may hold values from -1.5 to 1.5
- gain_attn: bfloat16 [768], P('shard'), may hold values from 0.5 to 1.5
- shift_attn: bfloat16 [768], P('shard'), may hold values from -3 to 3
- bias_in: bfloat16 [3072], P('shard'), may hold values from -1.5 to 1.5
- bias_down: bfloat16 [768], P('shard'), may hold values from -1.5 to 1.5
- gain_ffn: bfloat16 [768], P('shard'), may hold values from 0.5 to 1.5
- shift_ffn: bfloat16 [768], P('shard'), may hold values from -3 to 3
Outputs:
- layer_out: bfloat16 [8, 1536, 768], P('shard', 'ctx')
- grad_tokens: float32 [8, 1536, 768], P('shard', 'ctx')
- grad_w_qkv: float32 [768, 2304], P('shard')
- grad_w_out: float32 [768, 768], P('shard')
- grad_w_in: float32 [768, 3072], P('shard')
- grad_w_down: float32 [3072, 768], P('shard')
- grad_bias_query: float32 [768], P('shard')
- grad_bias_value: float32 [768], P('shard')
- grad_bias_out: float32 [768], P('shard')
- grad_gain_attn: float32 [768], P('shard')
- grad_shift_attn: float32 [768], P('shard')
- grad_bias_in: float32 [3072], P('shard')
- grad_bias_down: float32 [768], P('shard')
- grad_gain_ffn: float32 [768], P('shard')
- grad_shift_ffn: float32 [768], P('shard')
Inputs may be any that keep to these rules, and one draw needn't show every extreme that they name: `doc_lengths`: each row holds a sequence's document lengths in order, summing to 1536: either 2 to 4 nonzero lengths of at least 192 tokens each followed by zeros, or one document of 1536 tokens followed by zeros. In every draw at least one sequence is a single document.
All inputs are finite; a program needn't handle non-finite values.
Results may differ from a plain program's by a relative error of at most 0.02.
Values may be sent and summed in bfloat16 or wider, within the bound.
A program may use at most 128 MiB of HBM per device.

v0:
```python
import jax
import jax.numpy as jnp
from jax import lax
from jax.sharding import PartitionSpec as P

HEADS = 12
HEAD = 64


epsilon = 1e-12
scale_attn = 0.125


def layer_norm(values, gain, shift):
    center = values - jnp.mean(values, axis=-1, keepdims=True)
    spread = jnp.mean(center * center, axis=-1, keepdims=True)
    return center * lax.rsqrt(spread + epsilon) * gain + shift


def gelu_exact(values):
    return jax.nn.gelu(values, approximate=False)


def segment_ids(counts, length):
    places = jnp.arange(length, dtype=jnp.int32)
    first_end = counts[0]
    second_end = first_end + counts[1]
    third_end = second_end + counts[2]
    return (
        (places >= first_end).astype(jnp.int32)
        + (places >= second_end).astype(jnp.int32)
        + (places >= third_end).astype(jnp.int32)
    )


def split_heads(values):
    return values.reshape(values.shape[0], HEADS, HEAD).transpose(1, 0, 2)


def join_heads(values):
    return values.transpose(1, 0, 2).reshape(values.shape[1], HEADS * HEAD)


def head_forward(query_h, key_h, value_h, match_mask):
    scores = (
        jnp.einsum("qd,kd->qk", query_h, key_h, preferred_element_type=jnp.float32) * scale_attn
    )
    scores = jnp.where(match_mask, scores, -1000000000.0)
    maximum = jnp.max(scores, axis=-1, keepdims=True)
    exp_terms = jnp.exp(scores - maximum)
    total = jnp.sum(exp_terms, axis=-1, keepdims=True)
    weights_soft = (exp_terms / total).astype(jnp.bfloat16)
    mixed = jnp.dot(weights_soft, value_h, preferred_element_type=jnp.float32)
    return (mixed, (maximum + jnp.log(total))[:, 0])


def head_backward(query_h, key_h, value_h, dctx_h, log_total, match_mask):
    scores = (
        jnp.einsum("qd,kd->qk", query_h, key_h, preferred_element_type=jnp.float32) * scale_attn
    )
    probs = jnp.where(match_mask, jnp.exp(scores - log_total[:, None]), 0.0)
    grad_probs = jnp.einsum("qd,kd->qk", dctx_h, value_h, preferred_element_type=jnp.float32)
    grad_value = jnp.einsum(
        "qk,qd->kd", probs.astype(jnp.bfloat16), dctx_h, preferred_element_type=jnp.float32
    )
    inner = jnp.sum(probs * grad_probs, axis=-1, keepdims=True)
    grad_scores = (probs * (grad_probs - inner) * scale_attn).astype(jnp.bfloat16)
    grad_query = jnp.dot(grad_scores, key_h, preferred_element_type=jnp.float32)
    grad_key = jnp.einsum("qk,qd->kd", grad_scores, query_h, preferred_element_type=jnp.float32)
    return (grad_query, grad_key, grad_value)


def column_sums(values):
    return jnp.sum(values.astype(jnp.float32), axis=0)


def local(
    tokens,
    cotangent,
    doc_lengths,
    w_qkv,
    w_out,
    w_in,
    w_down,
    bias_query,
    bias_value,
    bias_out,
    gain_attn,
    shift_attn,
    bias_in,
    bias_down,
    gain_ffn,
    shift_ffn,
):
    gathered = (
        lax.all_gather(w_qkv, "shard", axis=0, tiled=True),
        lax.all_gather(w_out, "shard", axis=0, tiled=True),
        lax.all_gather(w_in, "shard", axis=0, tiled=True),
        lax.all_gather(w_down, "shard", axis=0, tiled=True),
        lax.all_gather(bias_query, "shard", axis=0, tiled=True),
        lax.all_gather(bias_value, "shard", axis=0, tiled=True),
        lax.all_gather(bias_out, "shard", axis=0, tiled=True),
        lax.all_gather(gain_attn, "shard", axis=0, tiled=True),
        lax.all_gather(shift_attn, "shard", axis=0, tiled=True),
        lax.all_gather(bias_in, "shard", axis=0, tiled=True),
        lax.all_gather(bias_down, "shard", axis=0, tiled=True),
        lax.all_gather(gain_ffn, "shard", axis=0, tiled=True),
        lax.all_gather(shift_ffn, "shard", axis=0, tiled=True),
    )
    mat_qkv, mat_out, mat_in, mat_down = (gathered[0], gathered[1], gathered[2], gathered[3])
    vec_query, vec_value, vec_out, gain_a, shift_a, vec_in, vec_down, gain_f, shift_f = [
        piece.astype(jnp.float32) for piece in gathered[4:]
    ]
    rows = tokens.shape[1]
    width = tokens.shape[2]
    inputs = tokens[0]
    length = rows * lax.axis_size("ctx")
    all_ids = segment_ids(doc_lengths[0], length)
    own_ids = lax.dynamic_slice_in_dim(all_ids, lax.axis_index("ctx") * rows, rows)
    match_mask = own_ids[:, None] == all_ids[None, :]
    projected = jnp.dot(inputs, mat_qkv, preferred_element_type=jnp.float32)
    query = (projected[:, :width] + vec_query).astype(jnp.bfloat16)
    key_local = projected[:, width : 2 * width].astype(jnp.bfloat16)
    value_local = (projected[:, 2 * width :] + vec_value).astype(jnp.bfloat16)
    key_all, value_all = (
        lax.all_gather(key_local, "ctx", axis=0, tiled=True),
        lax.all_gather(value_local, "ctx", axis=0, tiled=True),
    )
    query_heads = split_heads(query)
    key_heads = split_heads(key_all)
    value_heads = split_heads(value_all)
    mixed, log_total = lax.map(
        lambda items: head_forward(items[0], items[1], items[2], match_mask),
        (query_heads, key_heads, value_heads),
    )
    context = join_heads(mixed).astype(jnp.bfloat16)
    resid_attn = inputs.astype(jnp.float32) + (
        jnp.dot(context, mat_out, preferred_element_type=jnp.float32) + vec_out
    )
    hidden = layer_norm(resid_attn, gain_a, shift_a)
    hidden_low = hidden.astype(jnp.bfloat16)
    gate = jnp.dot(hidden_low, mat_in, preferred_element_type=jnp.float32) + vec_in
    active = gelu_exact(gate).astype(jnp.bfloat16)
    resid_ffn = hidden + (jnp.dot(active, mat_down, preferred_element_type=jnp.float32) + vec_down)
    layer_out = layer_norm(resid_ffn, gain_f, shift_f).astype(jnp.bfloat16)
    regathered = (
        lax.all_gather(w_qkv, "shard", axis=0, tiled=True),
        lax.all_gather(w_out, "shard", axis=0, tiled=True),
        lax.all_gather(w_in, "shard", axis=0, tiled=True),
        lax.all_gather(w_down, "shard", axis=0, tiled=True),
    )
    mat_qkv, mat_out, mat_in, mat_down = (
        regathered[0],
        regathered[1],
        regathered[2],
        regathered[3],
    )
    upstream = cotangent[0].astype(jnp.float32)
    _, norm_ffn_back = jax.vjp(layer_norm, resid_ffn, gain_f, shift_f)
    grad_resid_ffn, g_gain_f, g_shift_f = norm_ffn_back(upstream)
    d_ffn = grad_resid_ffn.astype(jnp.bfloat16)
    g_down = jnp.einsum("tf,td->fd", active, d_ffn, preferred_element_type=jnp.float32)
    g_bdown = column_sums(d_ffn)
    d_active = jnp.einsum("td,fd->tf", d_ffn, mat_down, preferred_element_type=jnp.float32)
    _, gelu_back = jax.vjp(gelu_exact, gate)
    d_gate = gelu_back(d_active)[0].astype(jnp.bfloat16)
    g_in = jnp.einsum("td,tf->df", hidden_low, d_gate, preferred_element_type=jnp.float32)
    g_bin = column_sums(d_gate)
    d_hidden = grad_resid_ffn + jnp.einsum(
        "tf,df->td", d_gate, mat_in, preferred_element_type=jnp.float32
    )
    _, norm_attn_back = jax.vjp(layer_norm, resid_attn, gain_a, shift_a)
    grad_resid_attn, g_gain_a, g_shift_a = norm_attn_back(d_hidden)
    d_attn = grad_resid_attn.astype(jnp.bfloat16)
    g_out = jnp.einsum("tc,td->cd", context, d_attn, preferred_element_type=jnp.float32)
    g_bout = column_sums(d_attn)
    d_context = jnp.einsum("td,cd->tc", d_attn, mat_out, preferred_element_type=jnp.float32).astype(
        jnp.bfloat16
    )
    dctx_heads = split_heads(d_context)
    grad_query, grad_key, grad_value = lax.map(
        lambda items: head_backward(items[0], items[1], items[2], items[3], items[4], match_mask),
        (query_heads, key_heads, value_heads, dctx_heads, log_total),
    )
    key_terms = join_heads(grad_key)
    value_terms = join_heads(grad_value)
    key_summed, value_summed = (
        lax.psum_scatter(
            key_terms.astype(jnp.bfloat16), "ctx", scatter_dimension=0, tiled=True
        ).astype(jnp.float32),
        lax.psum_scatter(
            value_terms.astype(jnp.bfloat16), "ctx", scatter_dimension=0, tiled=True
        ).astype(jnp.float32),
    )
    d_query = join_heads(grad_query).astype(jnp.bfloat16)
    d_key = key_summed.astype(jnp.bfloat16)
    d_value = value_summed.astype(jnp.bfloat16)
    d_proj = jnp.concatenate([d_query, d_key, d_value], axis=1)
    g_qkv = jnp.einsum("td,te->de", inputs, d_proj, preferred_element_type=jnp.float32)
    g_query = column_sums(d_query)
    g_value = column_sums(d_value)
    grad_tokens = grad_resid_attn + jnp.einsum(
        "te,de->td", d_proj, mat_qkv, preferred_element_type=jnp.float32
    )
    group_parts = (
        lax.psum_scatter(
            g_qkv.astype(jnp.bfloat16), "shard", scatter_dimension=0, tiled=True
        ).astype(jnp.float32),
        lax.psum_scatter(
            g_out.astype(jnp.bfloat16), "shard", scatter_dimension=0, tiled=True
        ).astype(jnp.float32),
        lax.psum_scatter(
            g_in.astype(jnp.bfloat16), "shard", scatter_dimension=0, tiled=True
        ).astype(jnp.float32),
        lax.psum_scatter(
            g_down.astype(jnp.bfloat16), "shard", scatter_dimension=0, tiled=True
        ).astype(jnp.float32),
        lax.psum_scatter(
            g_query.astype(jnp.bfloat16), "shard", scatter_dimension=0, tiled=True
        ).astype(jnp.float32),
        lax.psum_scatter(
            g_value.astype(jnp.bfloat16), "shard", scatter_dimension=0, tiled=True
        ).astype(jnp.float32),
        lax.psum_scatter(
            g_bout.astype(jnp.bfloat16), "shard", scatter_dimension=0, tiled=True
        ).astype(jnp.float32),
        lax.psum_scatter(
            g_gain_a.astype(jnp.bfloat16), "shard", scatter_dimension=0, tiled=True
        ).astype(jnp.float32),
        lax.psum_scatter(
            g_shift_a.astype(jnp.bfloat16), "shard", scatter_dimension=0, tiled=True
        ).astype(jnp.float32),
        lax.psum_scatter(
            g_bin.astype(jnp.bfloat16), "shard", scatter_dimension=0, tiled=True
        ).astype(jnp.float32),
        lax.psum_scatter(
            g_bdown.astype(jnp.bfloat16), "shard", scatter_dimension=0, tiled=True
        ).astype(jnp.float32),
        lax.psum_scatter(
            g_gain_f.astype(jnp.bfloat16), "shard", scatter_dimension=0, tiled=True
        ).astype(jnp.float32),
        lax.psum_scatter(
            g_shift_f.astype(jnp.bfloat16), "shard", scatter_dimension=0, tiled=True
        ).astype(jnp.float32),
    )
    (
        p_qkv,
        p_out,
        p_in,
        p_down,
        p_query,
        p_value,
        p_bout,
        p_gain_a,
        p_shift_a,
        p_bin,
        p_bdown,
        p_gain_f,
        p_shift_f,
    ) = group_parts
    summed = (
        lax.psum(p_qkv.astype(jnp.bfloat16), "ctx").astype(jnp.float32),
        lax.psum(p_out.astype(jnp.bfloat16), "ctx").astype(jnp.float32),
        lax.psum(p_in.astype(jnp.bfloat16), "ctx").astype(jnp.float32),
        lax.psum(p_down.astype(jnp.bfloat16), "ctx").astype(jnp.float32),
        lax.psum(p_query.astype(jnp.bfloat16), "ctx").astype(jnp.float32),
        lax.psum(p_value.astype(jnp.bfloat16), "ctx").astype(jnp.float32),
        lax.psum(p_bout.astype(jnp.bfloat16), "ctx").astype(jnp.float32),
        lax.psum(p_gain_a.astype(jnp.bfloat16), "ctx").astype(jnp.float32),
        lax.psum(p_shift_a.astype(jnp.bfloat16), "ctx").astype(jnp.float32),
        lax.psum(p_bin.astype(jnp.bfloat16), "ctx").astype(jnp.float32),
        lax.psum(p_bdown.astype(jnp.bfloat16), "ctx").astype(jnp.float32),
        lax.psum(p_gain_f.astype(jnp.bfloat16), "ctx").astype(jnp.float32),
        lax.psum(p_shift_f.astype(jnp.bfloat16), "ctx").astype(jnp.float32),
    )
    return (
        layer_out[None],
        grad_tokens[None],
        summed[0],
        summed[1],
        summed[2],
        summed[3],
        summed[4],
        summed[5],
        summed[6],
        summed[7],
        summed[8],
        summed[9],
        summed[10],
        summed[11],
        summed[12],
    )


def solution(mesh):
    return jax.shard_map(
        local,
        mesh=mesh,
        in_specs=(
            P("shard", "ctx", None),
            P("shard", "ctx", None),
            P("shard", None),
            P("shard", None),
            P("shard", None),
            P("shard", None),
            P("shard", None),
            P("shard"),
            P("shard"),
            P("shard"),
            P("shard"),
            P("shard"),
            P("shard"),
            P("shard"),
            P("shard"),
            P("shard"),
        ),
        out_specs=(
            P("shard", "ctx", None),
            P("shard", "ctx", None),
            P("shard", None),
            P("shard", None),
            P("shard", None),
            P("shard", None),
            P("shard"),
            P("shard"),
            P("shard"),
            P("shard"),
            P("shard"),
            P("shard"),
            P("shard"),
            P("shard"),
            P("shard"),
        ),
        check_vma=False,
    )
```

profile of v0, /device:TPU:0, one launch (start us, length us, event | category | flops | bytes accessed | tf_op | source)
XLA Modules:
  0.0 827.2 jit_solution(8002101448332740058)
XLA Ops:
  15.8 26.0 %all-reduce.18 = (bf16[768]{0:T(1024)(128)(2,1)S(1)}, bf16[768]{0:T(1024)(128)(2,1)S(1)}, bf16[768]{0:T(1024)(128)(2,1)}, bf16[768]{0:T(1024)(128)(2,1)}, bf16[7...) all-reduce(bf16[768]{0:T(1024)(128)(2,1)S(1)} %dynamic-update-slice, ...), channel_id=1, replica_groups=mesh['shard'=8,'ctx'=4] {'shard'}, use_global_device_ids=true, to_apply=%add | all-reduce | flops 5376 | bytes 21504
  41.9 5.0 all-gather.8.cloned.1.call-done
  46.8 3.7 fusion.64
  62.2 8.9 %all-gather = bf16[8,1,384]{2,1,0:T(2,128)(2,1)S(1)} all-gather(bf16[1,1,384]{2,1,0:T(2,128)(2,1)S(1)} %reshape.197), channel_id=1, replica_groups=mesh['shard'=8,'ctx'=4] {'shard'}, dimensions={0}, use_global_device_ids=true | all-gather | bytes 6912 | tf_op jit(solution)/shard_map/all_gather | solution.py:105
  74.6 27.7 %all-gather.12.cloned.1.call-done = bf16[1536,768]{1,0:T(8,128)(2,1)} async-done(((bf16[384,768]{1,0:T(8,128)(2,1)}), bf16[1536,768]{1,0:T(8,128)(2,1)}) %all-gather.12.cloned.1.call-update) | async-done | bytes 2359312 | tf_op jit(solution)/shard_map/all_gather | solution.py:127
  102.3 2.8 copy.50
  105.2 3.9 copy.53
  109.1 44.7 %all-gather.10.cloned.1.call-done = bf16[1536,768]{1,0:T(8,128)(2,1)} async-done(((bf16[384,768]{1,0:T(8,128)(2,1)}), bf16[1536,768]{1,0:T(8,128)(2,1)}) %all-gather.10.cloned.1.call-update) | async-done | bytes 2359312 | tf_op jit(solution)/shard_map/all_gather | solution.py:126
  153.8 2.8 copy.49
  156.7 4.0 copy.52
  161.6 74.9 %while.28 = (s32[]{:T(128)}, bf16[12,384,64]{1,2,0:T(8,128)(2,1)}, f32[12,384]{1,0:T(8,128)}, bf16[12,384,64]{2,1,0:T(8,128)(2,1)S(1)}, bf16[12,1536,64]{2,1,0:T...) while((s32[]{:T(128)}, bf16[12,384,64]{1,2,0:T(8,128)(2,1)}, ...), condition=%wide.region_3.4_spmd.clone, body=%wide.region_0.3_spmd.clone.sunk | while | flops 156302976 | bytes 8091753 | solution.py:132
  165.6 2.3 fusion.123
  171.8 2.3 fusion.123
  178.0 2.3 fusion.123
  184.3 2.3 fusion.123
  190.5 2.3 fusion.123
  196.8 2.3 fusion.123
  203.0 2.3 fusion.123
  209.2 2.3 fusion.123
  215.5 2.3 fusion.123
  221.7 2.3 fusion.123
  227.9 2.3 fusion.123
  234.2 2.3 fusion.123
  236.5 2.8 fusion.81
  239.7 15.6 %multiply_convert_fusion.1 = (bf16[384,3072]{1,0:T(8,128)(2,1)}, f32[384,3072]{1,0:T(8,128)}, f32[384,3072]{1,0:T(8,128)}) fusion(f32[3072]{0:T(1024)S(1)} %bitcast.164, bf16[768,3072]{1,0:T(8,128)(2,1)} %all-gather.16.cloned.1.call-done, f32[384,768]{1,0:T(8,128)S(1)} %get-tuple-element.338, f32[768]{0:T(1024)S(1)} %copy-done.27, f32[768]{0:T(1024)S(1)} %copy-done.18, ...), kind=kOutput, calls=%fused_computation.60 | convolution fusion | flops 1891270656 | bytes 17716224 | tf_op jit(solution)/shard_map/dot_general | solution.py:142
  255.3 4.6 all-gather.18.cloned.1.call-done
  259.9 5.3 fusion.82
  268.0 6.5 fusion.73
  274.6 2.9 multiply_reduce_fusion.1
  283.8 125.6 %while.29 = (s32[]{:T(128)}, bf16[12,384,64]{1,2,0:T(8,128)(2,1)}, bf16[12,1536,64]{1,2,0:T(8,128)(2,1)}, bf16[12,1536,64]{1,2,0:T(8,128)(2,1)}, bf16[12,384,64]...) while((s32[]{:T(128)}, bf16[12,384,64]{1,2,0:T(8,128)(2,1)}, ...), condition=%wide.region_14.15_spmd.clone, body=%wide.region_12.14_spmd.clone.sunk | while | flops 383975040 | bytes 20075128 | solution.py:181
  409.4 4.3 copy.60
  413.7 4.3 copy.62
  418.1 43.8 %reduce-scatter.19.cloned.1.call-done = bf16[384,768]{1,0:T(8,128)(2,1)} async-done(((bf16[1536,768]{1,0:T(8,128)(2,1)}), bf16[384,768]{1,0:T(8,128)(2,1)}) %reduce-scatter.19.cloned.1.call-update) | async-done | bytes 589840
  464.0 47.8 %reduce-scatter.21.cloned.1.call-done = bf16[384,768]{1,0:T(8,128)(2,1)} async-done(((bf16[1536,768]{1,0:T(8,128)(2,1)}), bf16[384,768]{1,0:T(8,128)(2,1)}) %reduce-scatter.21.cloned.1.call-update) | async-done | bytes 589840
  514.0 5.3 fusion.51
  519.3 5.8 copy.64
  525.2 2.9 convolution_convert_fusion.3
  528.3 6.6 convolution_convert_fusion
  535.6 7.3 convolution_convert_fusion.1
  543.1 29.8 %reduce-scatter.23.cloned.1.call-done = bf16[96,2304]{1,0:T(8,128)(2,1)} async-done(((bf16[768,2304]{1,0:T(8,128)(2,1)}), bf16[96,2304]{1,0:T(8,128)(2,1)}) %reduce-scatter.23.cloned.1.call-update) | async-done | bytes 442384
  574.9 38.4 %reduce-scatter.13.cloned.1.call-done = bf16[96,768]{1,0:T(8,128)(2,1)} async-done(((bf16[768,768]{1,0:T(8,128)(2,1)}), bf16[96,768]{1,0:T(8,128)(2,1)}) %reduce-scatter.13.cloned.1.call-update) | async-done | bytes 147472 | tf_op jit(solution)/shard_map/reduce_scatter | solution.py:209
  613.3 57.8 %reduce-scatter.17.cloned.1.call-done = bf16[384,768]{1,0:T(8,128)(2,1)} async-done(((bf16[3072,768]{1,0:T(8,128)(2,1)}), bf16[384,768]{1,0:T(8,128)(2,1)}) %reduce-scatter.17.cloned.1.call-update) | async-done | bytes 589840 | tf_op jit(solution)/shard_map/reduce_scatter | solution.py:215
  671.1 57.2 %reduce-scatter.15.cloned.1.call-done = bf16[96,3072]{1,0:T(8,128)(2,1)} async-done(((bf16[768,3072]{1,0:T(8,128)(2,1)}), bf16[96,3072]{1,0:T(8,128)(2,1)}) %reduce-scatter.15.cloned.1.call-update) | async-done | bytes 589840 | tf_op jit(solution)/shard_map/reduce_scatter | solution.py:212
  734.3 25.0 %all-reduce.17 = (bf16[768]{0:T(1024)(128)(2,1)S(1)}, bf16[768]{0:T(1024)(128)(2,1)S(1)}, bf16[768]{0:T(1024)(128)(2,1)S(1)}, bf16[768]{0:T(1024)(128)(2,1)S(1)}...) all-reduce(bf16[768]{0:T(1024)(128)(2,1)} %dynamic-update-slice.7, ...), channel_id=1, replica_groups=mesh['shard'=8,'ctx'=4] {'shard'}, use_global_device_ids=true, to_apply=%add.7 | all-reduce | flops 9984 | bytes 39936
  760.0 12.7 %all-reduce.19 = (bf16[96]{0:T(256)(128)(2,1)S(1)}, bf16[96]{0:T(256)(128)(2,1)S(1)}, bf16[96]{0:T(256)(128)(2,1)S(1)}, bf16[96]{0:T(256)(128)(2,1)S(1)}, bf16[9...) all-reduce(bf16[96]{0:T(256)(128)(2,1)S(1)} %dynamic-slice.9, ...), channel_id=1, replica_groups=mesh['shard'=8,'ctx'=4] {'ctx'}, use_global_device_ids=true, to_apply=%region_27.28 | all-reduce | flops 1152 | bytes 4608 | tf_op jit(solution)/shard_map/psum | solution.py:266
  778.5 5.2 fusion.55
  783.6 30.3 %all-reduce.23.cloned.1.call-done = (bf16[96,2304]{0,1:T(8,128)(2,1)}, bf16[96,768]{1,0:T(8,128)(2,1)}, bf16[96,3072]{1,0:T(8,128)(2,1)}, bf16[384,768]{1,0:T(8,128)(2,1)}) async-done(((bf16[96,2304]{0,1:T(8,128)(2,1)}, bf16[96,768]{1,0:T(8,128)(2,1)}, bf16[96,3072]{1,0:T(8,128)(2,1)}, bf16[384,768]{1,0:T(8,128)(2,1)}), (bf16[96,2304]{0,1:T(8,128)(2,1)}, bf16[96,768]{1,0:T(8,128)(2,1)}, ...) | async-done | bytes 1769488 | tf_op jit(solution)/shard_map/psum | solution.py:262
  813.9 2.2 convert_element_type.278
  (334 shorter events, 226.9 us)
Async XLA Ops:
  7.2 39.6 %all-gather.8.cloned.1.call-start = ((), (), s32[]{:S(2)}) async-start(), calls=%async_computation.6 | async-start | bytes 3981312 | tf_op jit(solution)/shard_map/all_gather | solution.py:96
  7.9 94.4 %all-gather.12.cloned.1.call-start = ((), (), s32[]{:S(2)}) async-start(), calls=%async_computation.8 | async-start | bytes 2949120 | tf_op jit(solution)/shard_map/all_gather | solution.py:127
  51.7 2.8 copy-start.26
  51.8 102.1 %all-gather.10.cloned.1.call-start = ((), (), s32[]{:S(2)}) async-start(), calls=%async_computation.7 | async-start | bytes 2949120 | tf_op jit(solution)/shard_map/all_gather | solution.py:126
  52.7 20.9 %copy-start.4 = (bf16[384,768]{1,0:T(8,128)(2,1)S(1)}, bf16[384,768]{1,0:T(8,128)(2,1)}, u32[]{:S(2)}) copy-start(bf16[384,768]{1,0:T(8,128)(2,1)} %get-tuple-element.331) | copy-start | bytes 1769476
  52.7 183.8 %all-gather.14.cloned.1.call-start = ((), (), s32[]{:S(2)}) async-start(), calls=%async_computation.9 | async-start | bytes 1327104 | tf_op jit(solution)/shard_map/all_gather | solution.py:97
  53.3 186.4 %all-gather.16.cloned.1.call-start = ((), (), s32[]{:S(2)}) async-start(), calls=%async_computation.10 | async-start | bytes 5308416 | tf_op jit(solution)/shard_map/all_gather | solution.py:98
  53.9 206.0 %all-gather.18.cloned.1.call-start = ((), (), s32[]{:S(2)}) async-start(), calls=%async_computation.11 | async-start | bytes 5308416 | tf_op jit(solution)/shard_map/all_gather | solution.py:99
  54.5 407.5 %reduce-scatter.19.cloned.1.call-start = ((), (), s32[]{:S(2)}) async-start(), calls=%async_computation.15 | async-start | bytes 2949120
  236.5 3.1 copy-start.3
  236.5 3.2 copy-start.18
  236.5 3.2 copy-start.21
  236.5 3.2 copy-start.27
  239.3 20.6 %copy-start.1 = (f32[384,768]{1,0:T(8,128)}, f32[384,768]{1,0:T(8,128)S(1)}, u32[]{:S(2)}) copy-start(f32[384,768]{1,0:T(8,128)S(1)} %get-tuple-element.338) | copy-start | bytes 3538948
  239.3 20.6 %copy-start.13 = (f32[384]{0:T(512)}, f32[384]{0:T(512)S(1)}, u32[]{:S(2)}) copy-start(f32[384]{0:T(512)S(1)} %broadcast_multiply_fusion.1) | copy-start | bytes 4612
  239.6 15.7 %copy-start.16 = (f32[384]{0:T(512)}, f32[384]{0:T(512)S(1)}, u32[]{:S(2)}) copy-start(f32[384]{0:T(512)S(1)} %multiply_reduce_fusion.4) | copy-start | bytes 4612
  239.6 15.7 %copy-start.23 = (f32[384]{0:T(512)}, f32[384]{0:T(512)S(1)}, u32[]{:S(2)}) copy-start(f32[384]{0:T(512)S(1)} %fusion.66) | copy-start | bytes 4612
  239.7 20.2 %copy-start.19 = (f32[768]{0:T(1024)S(1)}, f32[768]{0:T(1024)}, u32[]{:S(2)}) copy-start(f32[768]{0:T(1024)} %convert_element_type.248) | copy-start | bytes 9220
  239.7 20.2 %copy-start.28 = (f32[768]{0:T(1024)S(1)}, f32[768]{0:T(1024)}, u32[]{:S(2)}) copy-start(f32[768]{0:T(1024)} %convert_element_type.249) | copy-start | bytes 9220
  239.7 20.2 %copy-start.30 = (f32[768]{0:T(1024)S(1)}, f32[768]{0:T(1024)}, u32[]{:S(2)}) copy-start(f32[768]{0:T(1024)} %convert_element_type.253) | copy-start | bytes 9220
  259.9 5.7 copy-start
  259.9 5.7 copy-start.10
  259.9 8.0 copy-start.35
  265.6 1.6 copy-start.11
  265.6 2.4 copy-start.31
  266.7 7.9 slice-start
  268.0 6.6 copy-start.6
  268.0 6.6 copy-start.2
  268.0 6.6 copy-start.14
  268.0 6.6 copy-start.24
  268.0 6.6 slice-start.1
  274.5 2.9 copy-start.34
  274.6 2.9 copy-start.17
  277.5 1.8 copy-start.32
  413.7 98.1 %reduce-scatter.21.cloned.1.call-start = ((), (), s32[]{:S(2)}) async-start(), calls=%async_computation.16 | async-start | bytes 2949120
  418.1 154.8 %reduce-scatter.23.cloned.1.call-start = ((), (), s32[]{:S(2)}) async-start(), calls=%async_computation.17 | async-start | bytes 3981312
  525.1 88.2 %reduce-scatter.13.cloned.1.call-start = ((), (), s32[]{:S(2)}) async-start(), calls=%async_computation.12 | async-start | bytes 1327104 | tf_op jit(solution)/shard_map/reduce_scatter | solution.py:209
  528.0 143.0 %reduce-scatter.17.cloned.1.call-start = ((), (), s32[]{:S(2)}) async-start(), calls=%async_computation.14 | async-start | bytes 5308416 | tf_op jit(solution)/shard_map/reduce_scatter | solution.py:215
  535.0 0.7 copy-start.25
  535.0 0.7 copy-start.29
  535.0 193.3 %reduce-scatter.15.cloned.1.call-start = ((), (), s32[]{:S(2)}) async-start(), calls=%async_computation.13 | async-start | bytes 5308416 | tf_op jit(solution)/shard_map/reduce_scatter | solution.py:212
  543.0 187.9 %copy-start.33 = (bf16[96]{0:T(256)(128)(2,1)S(1)}, bf16[96]{0:T(256)(128)(2,1)}, u32[]{:S(2)}) copy-start(bf16[96]{0:T(256)(128)(2,1)} %param.35) | copy-start | bytes 580
  543.0 191.2 %copy-start.5 = (bf16[384,768]{1,0:T(8,128)(2,1)S(1)}, bf16[384,768]{1,0:T(8,128)(2,1)}, u32[]{:S(2)}) copy-start(bf16[384,768]{1,0:T(8,128)(2,1)} %reduce-scatter.21.cloned.1.call-done) | copy-start | bytes 1769476
  543.0 234.4 %copy-start.12 = (f32[384]{0:T(512)S(1)}, f32[384]{0:T(512)}, u32[]{:S(2)}) copy-start(f32[384]{0:T(512)} %copy-done.11) | copy-start | bytes 4612
  543.0 270.9 %all-reduce.23.cloned.1.call-start = ((), (), s32[]{:S(2)}) async-start(), calls=%async_computation.18 | async-start | bytes 3833856 | tf_op jit(solution)/shard_map/psum | solution.py:262
  729.0 49.5 %copy-start.7 = (bf16[384,768]{0,1:T(8,128)(2,1)S(1)}, bf16[384,768]{0,1:T(8,128)(2,1)}, u32[]{:S(2)}) copy-start(bf16[384,768]{0,1:T(8,128)(2,1)} %copy.61) | copy-start | bytes 1769476
  813.9 4.4 copy-start.8
  813.9 5.6 copy-start.9
  (3 other events, 1.9 us)
Sparse Core Ops, SparseCore 0:
  9.9 36.8 all-gather.7
  51.9 50.4 all-gather.11
  104.5 49.2 all-gather.9
  155.6 22.8 all-gather.13
  180.2 38.9 all-gather.15
  220.9 38.9 all-gather.17
  413.8 48.0 reduce-scatter.18
  464.2 47.5 reduce-scatter.20
  525.2 47.5 reduce-scatter.22
  576.5 36.7 reduce-scatter.12
  617.1 53.8 reduce-scatter.16
  674.4 53.8 reduce-scatter.14
  731.7 82.2 all-reduce.22
where the time goes:
time: 836 us; the launch traced here: 827 us
  waiting for transfers between devices  389 us (47%)
  matrix products  225 us (27%)
  local copies, waits for them, and re-layouts  86.5 us (10%)
  blocking collectives  72.6 us (9%)
  other arithmetic  34.3 us (4%)
  between operations  18.8 us (2%)
    unnamed x16, waiting for transfers between devices  124 us
    reduce_scatter x1, waiting for transfers between devices, local(): lax.psum_scatter(g_down.astype(jnp.bfloat16), 'shard', scatter_dimension=...  57.8 us
    reduce_scatter x1, waiting for transfers between devices, local(): lax.psum_scatter(g_in.astype(jnp.bfloat16), 'shard', scatter_dimension=0,...  57.2 us
    unnamed x2, blocking collectives  51 us
    all_gather x1, waiting for transfers between devices, local(): lax.all_gather(key_local, 'ctx', axis=0, tiled=True)  44.7 us
    unnamed x113, local copies, waits for them, and re-layouts  42.4 us
    reduce_scatter x1, waiting for transfers between devices, local(): lax.psum_scatter(g_out.astype(jnp.bfloat16), 'shard', scatter_dimension=0...  38.4 us
    psum x1, waiting for transfers between devices, local(): lax.psum(p_qkv.astype(jnp.bfloat16), 'ctx').astype(jnp.float32)  30.3 us
  transfers between devices with their start and end apart: 13, of which 11 were waited for; matrix products, arithmetic and copies ran while one was open for 20% of the time, Pallas kernels for 0%

commit v1 on v0

--- a/solution.py
+++ b/solution.py
@@ -1,6 +1,10 @@
+import functools
+
 import jax
 import jax.numpy as jnp
 from jax import lax
+from jax.experimental import pallas as pl
+from jax.experimental.pallas import tpu as pltpu
 from jax.sharding import PartitionSpec as P
 
 HEADS = 12
@@ -74,7 +78,7 @@
     return jnp.sum(values.astype(jnp.float32), axis=0)
 
 
-def local(
+def local_any(
     tokens,
     cotangent,
     doc_lengths,
@@ -292,9 +296,341 @@
     )
 
 
+QUERY_BLOCK = 256
+VMEM_BYTES = 56 * 1024 * 1024
+TN = (((0,), (0,)), ((), ()))
+NT = (((1,), (1,)), ((), ()))
+
+
+def dot(a, b, dims=(((1,), (0,)), ((), ()))):
+    return lax.dot_general(a, b, dims, preferred_element_type=jnp.float32)
+
+
+def attend_kernel(ids_row, ids_col, q_ref, k_ref, v_ref, ctx_ref, p_ref):
+    scores = dot(k_ref[...], q_ref[...] * jnp.bfloat16(0.125), TN)
+    scores = jnp.where(ids_col[...] == ids_row[...], scores, -1000000000.0)
+    maximum = jnp.max(scores, axis=0, keepdims=True)
+    terms = jnp.exp(scores - maximum)
+    total = jnp.sum(terms, axis=0, keepdims=True)
+    probs = (terms * (1.0 / total)).astype(jnp.bfloat16)
+    p_ref[0] = probs
+    ctx_ref[...] = dot(v_ref[...], probs).astype(jnp.bfloat16)
+
+
+def attend(ids, q, k, v):
+    width, length = q.shape
+    heads = width // HEAD
+    block = QUERY_BLOCK
+    row = pl.BlockSpec((HEAD, length), lambda h, b: (h, 0))
+    part = pl.BlockSpec((HEAD, block), lambda h, b: (h, b))
+    return pl.pallas_call(
+        attend_kernel,
+        grid=(heads, length // block),
+        in_specs=[
+            pl.BlockSpec((1, block), lambda h, b: (0, b)),
+            pl.BlockSpec((length, 1), lambda h, b: (0, 0)),
+            part,
+            row,
+            row,
+        ],
+        out_specs=[part, pl.BlockSpec((1, length, block), lambda h, b: (h, 0, b))],
+        out_shape=[
+            jax.ShapeDtypeStruct((width, length), jnp.bfloat16),
+            jax.ShapeDtypeStruct((heads, length, length), jnp.bfloat16),
+        ],
+        compiler_params=pltpu.CompilerParams(vmem_limit_bytes=VMEM_BYTES),
+        cost_estimate=pl.CostEstimate(
+            flops=heads * length * length * 256 * 4,
+            bytes_accessed=heads * length * length * 4,
+            transcendentals=heads * length * length,
+        ),
+        name="attend",
+    )(ids[None, :], ids[:, None], q, k, v)
+
+
+def attend_back_kernel(
+    q_ref, k_ref, v_ref, d_ref, ctx_ref, p_ref, dq_ref, dk_ref, dv_ref, dk_sum, dv_sum
+):
+    step = pl.program_id(1)
+
+    @pl.when(step == 0)
+    def _():
+        dk_sum[...] = jnp.zeros_like(dk_sum)
+        dv_sum[...] = jnp.zeros_like(dv_sum)
+
+    probs = p_ref[0]
+    d_ctx = d_ref[...]
+    inner = jnp.sum(
+        d_ctx.astype(jnp.float32) * ctx_ref[...].astype(jnp.float32), axis=0, keepdims=True
+    )
+    d_probs = dot(v_ref[...], d_ctx, TN)
+    d_scores = (probs.astype(jnp.float32) * (d_probs - inner)).astype(jnp.bfloat16)
+    dq_ref[...] = (dot(k_ref[...], d_scores) * 0.125).astype(jnp.bfloat16)
+    dk_sum[...] += dot(d_scores, q_ref[...], NT)
+    dv_sum[...] += dot(probs, d_ctx, NT)
+
+    @pl.when(step == pl.num_programs(1) - 1)
+    def _():
+        dk_ref[...] = (dk_sum[...].T * 0.125).astype(jnp.bfloat16)
+        dv_ref[...] = dv_sum[...].T.astype(jnp.bfloat16)
+
+
+def attend_back(q, k, v, d_ctx, ctx, probs):
+    width, length = q.shape
+    heads = width // HEAD
+    block = QUERY_BLOCK
+    row = pl.BlockSpec((HEAD, length), lambda h, b: (h, 0))
+    part = pl.BlockSpec((HEAD, block), lambda h, b: (h, b))
+    shape = jax.ShapeDtypeStruct((width, length), jnp.bfloat16)
+    return pl.pallas_call(
+        attend_back_kernel,
+        grid=(heads, length // block),
+        in_specs=[
+            part,
+            row,
+            row,
+            part,
+            part,
+            pl.BlockSpec((1, length, block), lambda h, b: (h, 0, b)),
+        ],
+        out_specs=[part, row, row],
+        out_shape=[shape, shape, shape],
+        scratch_shapes=[pltpu.VMEM((length, HEAD), jnp.float32)] * 2,
+        compiler_params=pltpu.CompilerParams(vmem_limit_bytes=VMEM_BYTES),
+        cost_estimate=pl.CostEstimate(
+            flops=heads * length * length * 256 * 10,
+            bytes_accessed=heads * length * length * 4,
+            transcendentals=0,
+        ),
+        name="attend_back",
+    )(q, k, v, d_ctx, ctx, probs)
+
+
+def swap(values, bit):
+    return lax.ppermute(values, "shard", [(i, i ^ bit) for i in range(8)])
+
+
+def place_kernel(*refs):
+    *pieces, whole, sems = refs
+    me = lax.axis_index("shard")
+    rows = pieces[0].shape[0]
+    half = rows // 2
+    copies = []
+    for core in (0, 1):
+        own, over_x, over_y, top, bottom = pieces[core * 5 : core * 5 + 5]
+        for piece, bits, shift in (
+            (own, 0, 0),
+            (over_x, 2, 0),
+            (over_y, 4, 0),
+            (top, 6, 0),
+            (bottom, 6, half),
+        ):
+            owner = flip(me, bits + core)
+            start = pl.multiple_of(owner * rows + shift, 16)
+            copies.append(
+                pltpu.make_async_copy(
+                    piece, whole.at[pl.ds(start, piece.shape[0])], sems.at[len(copies)]
+                )
+            )
+    for copy in copies:
+        copy.start()
+    for copy in copies:
+        copy.wait()
+
+
+def flip(index, bits):
+    result = index
+    for bit in (1, 2, 4):
+        if bits & bit:
+            held = lax.rem(index // bit, 2)
+            result = result + bit - 2 * bit * held
+    return result
+
+
+def gather_shard(piece):
+    rows, columns = piece.shape
+    half = rows // 2
+    over_x = swap(piece, 2)
+    over_y = swap(piece, 4)
+    top = swap(over_x[:half], 4)
+    bottom = swap(over_y[half:], 2)
+    near = [piece, over_x, over_y, top, bottom]
+    far = [swap(part, 1) for part in near]
+    return pl.pallas_call(
+        place_kernel,
+        in_specs=[pl.BlockSpec(memory_space=pl.ANY)] * 10,
+        out_specs=pl.BlockSpec(memory_space=pl.ANY),
+        out_shape=jax.ShapeDtypeStruct((8 * rows, columns), piece.dtype),
+        scratch_shapes=[pltpu.SemaphoreType.DMA((10,))],
+        cost_estimate=pl.CostEstimate(
+            flops=0, bytes_accessed=32 * rows * columns, transcendentals=0
+        ),
+        name="place_rows",
+    )(*near, *far)
+
+
+def add_low(a, b):
+    return (a.astype(jnp.float32) + b.astype(jnp.float32)).astype(jnp.bfloat16)
+
+
+def pick(values, index, axis):
+    return lax.dynamic_index_in_dim(values, index, axis, keepdims=False)
+
+
+def scatter_shard(whole):
+    me = lax.axis_index("shard")
+    core, x, y = me % 2, (me // 2) % 2, me // 4
+    rows, columns = whole.shape[0] // 8, whole.shape[1]
+    half = columns // 2
+    parts = whole.reshape(4, 2, rows, columns)
+    mine = add_low(pick(parts, core, 1), swap(pick(parts, 1 - core, 1), 1))
+    mine = mine.reshape(2, 2, rows, columns)
+    left, right = mine[..., :half], mine[..., half:]
+    left = add_low(pick(left, x, 1), swap(pick(left, 1 - x, 1), 2))
+    right = add_low(pick(right, y, 0), swap(pick(right, 1 - y, 0), 4))
+    left = add_low(pick(left, y, 0), swap(pick(left, 1 - y, 0), 4))
+    right = add_low(pick(right, x, 0), swap(pick(right, 1 - x, 0), 2))
+    return jnp.concatenate([left, right], axis=1)
+
+
+def local_fast(
+    tokens,
+    cotangent,
+    doc_lengths,
+    w_qkv,
+    w_out,
+    w_in,
+    w_down,
+    bias_query,
+    bias_value,
+    bias_out,
+    gain_attn,
+    shift_attn,
+    bias_in,
+    bias_down,
+    gain_ffn,
+    shift_ffn,
+):
+    blocks = lax.axis_size("ctx")
+    place = lax.axis_index("ctx")
+    inputs = tokens[0]
+    rows, width = inputs.shape
+    length = rows * blocks
+    share = width // blocks
+    vectors = [
+        bias_query,
+        bias_value,
+        bias_out,
+        gain_attn,
+        shift_attn,
+        bias_in,
+        bias_down,
+        gain_ffn,
+        shift_ffn,
+    ]
+    sizes = [vector.shape[0] for vector in vectors]
+
+    tokens_all = lax.all_gather(inputs, "ctx", axis=0, tiled=True)
+    qkv_part = lax.dynamic_index_in_dim(
+        w_qkv.reshape(w_qkv.shape[0], 3, blocks, share), place, 2, keepdims=False
+    ).reshape(w_qkv.shape[0], 3 * share)
+    mat_qkv = gather_shard(qkv_part)
+    packed = lax.all_gather(jnp.concatenate(vectors), "shard", axis=0, tiled=False)
+    mat_out = gather_shard(w_out)
+    mat_in = gather_shard(w_in)
+    mat_down = gather_shard(w_down)
+    edges = [sum(sizes[:i]) for i in range(len(sizes) + 1)]
+    vec_query, vec_value, vec_out, gain_a, shift_a, vec_in, vec_down, gain_f, shift_f = [
+        packed[:, edges[i] : edges[i + 1]].reshape(-1).astype(jnp.float32)
+        for i in range(len(sizes))
+    ]
+
+    ids = segment_ids(doc_lengths[0], length)
+    bias_q = lax.dynamic_slice_in_dim(vec_query, place * share, share)
+    bias_v = lax.dynamic_slice_in_dim(vec_value, place * share, share)
+    proj = lax.dot_general(
+        mat_qkv, tokens_all, (((0,), (1,)), ((), ())), preferred_element_type=jnp.float32
+    )
+    query = (proj[:share] + bias_q[:, None]).astype(jnp.bfloat16)
+    key = proj[share : 2 * share].astype(jnp.bfloat16)
+    value = (proj[2 * share :] + bias_v[:, None]).astype(jnp.bfloat16)
+    mixed, probs = attend(ids, query, key, value)
+    context = lax.all_to_all(mixed, "ctx", 1, 0, tiled=True)
+
+    resid_attn = inputs.astype(jnp.float32) + (dot(context, mat_out, TN) + vec_out)
+    hidden = layer_norm(resid_attn, gain_a, shift_a)
+    hidden_low = hidden.astype(jnp.bfloat16)
+    gate = dot(hidden_low, mat_in) + vec_in
+    active = gelu_exact(gate).astype(jnp.bfloat16)
+    resid_ffn = hidden + (dot(active, mat_down) + vec_down)
+    layer_out = layer_norm(resid_ffn, gain_f, shift_f).astype(jnp.bfloat16)
+
+    upstream = cotangent[0].astype(jnp.float32)
+    _, norm_ffn_back = jax.vjp(layer_norm, resid_ffn, gain_f, shift_f)
+    grad_resid_ffn, g_gain_f, g_shift_f = norm_ffn_back(upstream)
+    d_ffn = grad_resid_ffn.astype(jnp.bfloat16)
+    g_down = dot(active, d_ffn, TN).astype(jnp.bfloat16)
+    g_bdown = column_sums(d_ffn)
+    d_active = dot(d_ffn, mat_down, NT)
+    _, gelu_back = jax.vjp(gelu_exact, gate)
+    d_gate = gelu_back(d_active)[0].astype(jnp.bfloat16)
+    g_in = dot(hidden_low, d_gate, TN).astype(jnp.bfloat16)
+    g_bin = column_sums(d_gate)
+    d_hidden = grad_resid_ffn + dot(d_gate, mat_in, NT)
+    _, norm_attn_back = jax.vjp(layer_norm, resid_attn, gain_a, shift_a)
+    grad_resid_attn, g_gain_a, g_shift_a = norm_attn_back(d_hidden)
+    d_attn = grad_resid_attn.astype(jnp.bfloat16)
+    g_out = dot(context, d_attn).astype(jnp.bfloat16)
+    g_bout = column_sums(d_attn)
+    d_context = dot(mat_out, d_attn, NT).astype(jnp.bfloat16)
+
+    d_context, g_down, g_in, g_out = lax.optimization_barrier((d_context, g_down, g_in, g_out))
+    d_mixed = lax.all_to_all(d_context, "ctx", 0, 1, tiled=True)
+    s_down = scatter_shard(g_down)
+    s_in = scatter_shard(g_in)
+    s_out = scatter_shard(g_out)
+    d_query, d_key, d_value = attend_back(query, key, value, d_mixed, mixed, probs)
+    d_proj = jnp.concatenate([d_query, d_key, d_value], axis=0)
+    spread = dot(d_proj, mat_qkv, (((0,), (1,)), ((), ()))).astype(jnp.bfloat16)
+    summed_tokens = lax.psum_scatter(spread, "ctx", scatter_dimension=0, tiled=True)
+    grad_tokens = grad_resid_attn + summed_tokens.astype(jnp.float32)
+    g_qkv = lax.dot_general(
+        tokens_all, d_proj, (((0,), (1,)), ((), ())), preferred_element_type=jnp.float32
+    ).astype(jnp.bfloat16)
+    s_qkv = scatter_shard(g_qkv)
+    all_qkv = lax.all_gather(s_qkv.reshape(-1, 3, share), "ctx", axis=2, tiled=True)
+    out_qkv = all_qkv.reshape(-1, 3 * width).astype(jnp.float32)
+
+    def widen(part):
+        whole = jnp.zeros((width,), jnp.float32)
+        return lax.dynamic_update_slice_in_dim(whole, part, place * share, 0)
+
+    g_query = widen(jnp.sum(d_query.astype(jnp.float32), axis=1))
+    g_value = widen(jnp.sum(d_value.astype(jnp.float32), axis=1))
+    small = [g_query, g_value, g_bout, g_gain_a, g_shift_a, g_bin, g_bdown, g_gain_f, g_shift_f]
+    small = jnp.concatenate([part.reshape(8, -1) for part in small], axis=1)
+    small = lax.psum(small, ("shard", "ctx"))
+    small = lax.dynamic_index_in_dim(small, lax.axis_index("shard"), 0, keepdims=False)
+    small = [small[edges[i] : edges[i + 1]] for i in range(len(sizes))]
+    out_down = lax.psum(s_down, "ctx").astype(jnp.float32)
+    out_in = lax.psum(s_in, "ctx").astype(jnp.float32)
+    out_out = lax.psum(s_out, "ctx").astype(jnp.float32)
+    return (
+        layer_out[None],
+        grad_tokens[None],
+        out_qkv,
+        out_out,
+        out_in,
+        out_down,
+        *small,
+    )
+
+
 def solution(mesh):
+    sizes = (mesh.shape["shard"], mesh.shape["ctx"])
+    chosen = local_fast if sizes == (8, 4) else local_any
     return jax.shard_map(
-        local,
+        chosen,
         mesh=mesh,
         in_specs=(
             P("shard", "ctx", None),

time: 836 us -> 743 us (0.89)
  Pallas kernels: 0 us -> 406 us
  waiting for transfers between devices: 389 us -> 50 us
  matrix products: 225 us -> 47.4 us
  starting transfers between devices: 0.78 us -> 53.2 us
  local copies, waits for them, and re-layouts: 86.5 us -> 35.1 us
  blocking collectives: 72.6 us -> 96.9 us
    pallas_call x0 -> x6, Pallas kernels: none -> 406 us  [the longest x4 356 us: gather_shard(): pl.pallas_call(place_kernel, in_specs=[pl.BlockSpec(memory_space=pl.ANY)]...]
    dot_general x96 -> x12, matrix products: 225 us -> 47.4 us  [the longest x10 39.7 us: dot(): return lax.dot_general(a, b, dims, preferred_element_type=jnp.float32)]
    reduce_scatter x3 -> x1, waiting for transfers between devices: 153 us -> 0.01 us  [local_fast(): lax.psum_scatter(spread, 'ctx', scatter_dimension=0, tiled=True)]
    unnamed x16 -> x3, waiting for transfers between devices: 124 us -> 0.71 us
    all_gather x6 -> x1, waiting for transfers between devices: 82 us -> 0.01 us  [local_fast(): tokens_all = lax.all_gather(inputs, 'ctx', axis=0, tiled=True)]
    unnamed x2 -> x0, blocking collectives: 51 us -> none
    ppermute x0 -> x56, waiting for transfers between devices: none -> 49.3 us  [swap(): return lax.ppermute(values, 'shard', [(i, i ^ bit) for i in range(8)])]
    all_gather x1 -> x2, blocking collectives: 8.91 us -> 55.7 us  [the longest x1 28.7 us: local_fast(): lax.all_gather(s_qkv.reshape(-1, 3, share), 'ctx', axis=2, tiled=True)]
  transfers between devices with their start and end apart: 13 -> 61, of which waited for: 11 -> 16; matrix products, arithmetic and copies ran while one was open for 20% -> 9% of each run, Pallas kernels for 0% -> 55%
where the time goes in v1:
time: 743 us; the launch traced here: 736 us
  Pallas kernels  406 us (55%)
  blocking collectives  96.9 us (13%)
  starting transfers between devices  53.2 us (7%)
  waiting for transfers between devices  50 us (7%)
  matrix products  47.4 us (6%)
  local copies, waits for them, and re-layouts  35.1 us (5%)
  other arithmetic  30 us (4%)
  between operations  17.4 us (2%)
    pallas_call x4, Pallas kernels, gather_shard(): pl.pallas_call(place_kernel, in_specs=[pl.BlockSpec(memory_space=pl.ANY)]...  356 us
    ppermute x56, waiting for transfers between devices, swap(): return lax.ppermute(values, 'shard', [(i, i ^ bit) for i in range(8)])  49.3 us
    ppermute x56, starting transfers between devices, swap(): return lax.ppermute(values, 'shard', [(i, i ^ bit) for i in range(8)])  42.9 us
    psum x1, blocking collectives, local_fast(): small = lax.psum(small, ('shard', 'ctx'))  41.2 us
    dot_general x10, matrix products, dot(): return lax.dot_general(a, b, dims, preferred_element_type=jnp.float32)  39.7 us
    all_gather x1, blocking collectives, local_fast(): lax.all_gather(s_qkv.reshape(-1, 3, share), 'ctx', axis=2, tiled=True)  28.7 us
    all_gather x1, blocking collectives, local_fast(): lax.all_gather(jnp.concatenate(vectors), 'shard', axis=0, tiled=False)  27 us
    pallas_call x1, Pallas kernels, attend(): pl.pallas_call(attend_kernel, grid=(heads, length // block), in_specs=[pl...  25.1 us
  transfers between devices with their start and end apart: 61, of which 16 were waited for; matrix products, arithmetic and copies ran while one was open for 9% of the time, Pallas kernels for 55%

profile of v1, /device:TPU:0, one launch (start us, length us, event | category | flops | bytes accessed | tf_op | source)
XLA Modules:
  0.0 735.8 jit_solution(4963428268351856541)
XLA Ops:
  10.4 3.0 collective-permute-start
  16.7 2.0 collective-permute-start.2
  18.7 2.5 collective-permute-start.3
  24.0 1.8 collective-permute-start.19
  26.1 1.9 collective-permute-start.28
  28.1 1.8 convert_add_fusion.8.ids_col
  30.0 27.0 %all-gather.2 = bf16[8,1,1152]{2,1,0:T(2,128)(2,1)S(1)} all-gather(bf16[1,1,1152]{2,1,0:T(2,128)(2,1)S(1)} %reshape.405), channel_id=3, replica_groups=mesh['shard'=8,'ctx'=4] {'shard'}, dimensions={0}, use_global_device_ids=true | all-gather | bytes 20736 | tf_op jit(solution)/shard_map/all_gather | solution.py:538
  63.5 31.0 %place_rows.4 = bf16[768,576]{1,0:T(8,128)(2,1)} custom-call(bf16[96,576]{1,0:T(8,128)(2,1)} %copy-done.15, bf16[96,576]{1,0:T(8,128)(2,1)} %copy-done.23, bf16[96,576]{1,0:T(8,128)(2,1)} %copy-done.24, bf16[48,576]{1,0:T(8,128)(2,1)} %copy-done.33, bf16[48,576]{1,0:T(8,128)(2,1)} %copy-done.34, bf16[96,576]{1,0:T(8,128)(2,1)} %copy-done.27, ...), custom_call_target="tpu_custom_call" | custom-call | bytes 1769472 | tf_op jit(solution)/shard_map/place_rows/pallas_call | solution.py:459
  100.1 3.6 fusion.10
  110.9 3.5 collective-permute-done.20.refs_3_
  115.2 25.1 %attend.1 = (bf16[192,1536]{1,0:T(8,128)(2,1)}, bf16[3,1536,1536]{2,1,0:T(8,128)(2,1)}) custom-call(s32[1,1536]{1,0:T(1,128)} %fusion.49.ids_row, s32[1536,1]{1,0:T(8,128)} %convert_add_fusion.8.ids_col, bf16[192,1536]{1,0:T(8,128)(2,1)} %get-tuple-element.54.q_ref, bf16[192,1536]{1,0:T(8,128)(2,1)} %slice.244.k_ref, bf16[192,1536]{1,0:T(8,128)(2,1)} %get-tuple-element.53.v_ref), custom_call_target="tpu_custom_call" | custom-call | flops 7247757312 | bytes 28311552 | tf_op jit(solution)/shard_map/attend/pallas_call | solution.py:326
  140.3 2.0 copy.95
  142.2 4.9 all-to-all-start
  148.3 2.4 collective-permute-done.25.refs_8_
  157.5 36.9 %place_rows.5 = bf16[768,768]{1,0:T(8,128)(2,1)} custom-call(bf16[96,768]{1,0:T(8,128)(2,1)} %refs_0_.3, bf16[96,768]{1,0:T(8,128)(2,1)} %copy-done.16, bf16[96,768]{1,0:T(8,128)(2,1)} %copy-done.17, bf16[48,768]{1,0:T(8,128)(2,1)} %collective-permute-done.11.refs_3_, bf16[48,768]{1,0:T(8,128)(2,1)} %collective-permute-done.12.refs_4_, ...), custom_call_target="tpu_custom_call" | custom-call | bytes 2359296 | tf_op jit(solution)/shard_map/place_rows/pallas_call | solution.py:459
  194.4 144.1 %place_rows.6 = bf16[768,3072]{1,0:T(8,128)(2,1)} custom-call(bf16[96,3072]{1,0:T(8,128)(2,1)} %refs_0_.4, bf16[96,3072]{1,0:T(8,128)(2,1)} %copy-done.7, bf16[96,3072]{1,0:T(8,128)(2,1)} %copy-done.8, bf16[48,3072]{1,0:T(8,128)(2,1)} %copy-done.19, bf16[48,3072]{1,0:T(8,128)(2,1)} %collective-permute-done.21.refs_4_, ...), custom_call_target="tpu_custom_call" | custom-call | bytes 9437184 | tf_op jit(solution)/shard_map/place_rows/pallas_call | solution.py:459
  338.7 144.1 %place_rows.7 = bf16[3072,768]{1,0:T(8,128)(2,1)} custom-call(bf16[384,768]{1,0:T(8,128)(2,1)} %refs_0_.5, bf16[384,768]{1,0:T(8,128)(2,1)} %copy-done.5, bf16[384,768]{1,0:T(8,128)(2,1)} %copy-done.6, bf16[192,768]{1,0:T(8,128)(2,1)} %collective-permute-done.29.refs_3_, bf16[192,768]{1,0:T(8,128)(2,1)} %collective-permute-done.30.refs_4_, ...), custom_call_target="tpu_custom_call" | custom-call | bytes 9437184 | tf_op jit(solution)/shard_map/place_rows/pallas_call | solution.py:459
  485.2 13.6 %multiply_convert_fusion = (bf16[384,3072]{1,0:T(8,128)(2,1)S(1)}, f32[384,3072]{1,0:T(8,128)S(1)}, f32[384,3072]{1,0:T(8,128)}) fusion(f32[3072]{0:T(1024)S(1)} %copy-done.41, bf16[768,3072]{1,0:T(8,128)(2,1)S(1)} %copy-done.2, f32[384,768]{1,0:T(8,128)S(1)} %get-tuple-element.84, f32[768]{0:T(1024)S(1)} %copy-done.47, f32[768]{0:T(1024)S(1)} %copy-done.39, ...), kind=kOutput, calls=%fused_computation.10 | convolution fusion | flops 1891270656 | bytes 17716224 | tf_op jit(solution)/shard_map/dot_general | solution.py:306
  498.9 2.1 fusion.64
  503.4 4.3 convolution_convert_fusion.1
  507.7 6.0 convert_reduce_fusion
  513.7 2.9 multiply_reduce_fusion
  516.6 3.3 convolution_convert_fusion
  525.9 5.1 all-to-all-start.1
  533.2 3.2 dynamic-slice_bitcast_fusion
  536.4 1.7 collective-permute-start.42
  538.9 4.3 collective-permute-done.42
  544.8 2.8 collective-permute-done.43
  549.2 3.9 fusion.2
  555.5 2.2 fusion.1
  558.1 1.8 collective-permute-start.54
  560.4 9.3 %collective-permute-done.49 = bf16[2,96,1536]{2,1,0:T(8,128)(2,1)S(1)} collective-permute-done((bf16[2,96,1536]{2,1,0:T(8,128)(2,1)S(1)}, bf16[2,96,1536]{2,1,0:T(8,128)(2,1)S(1)}, u32[]{:S(2)}, u32[]{:S(2)}) %collective-permute-start.49) | collective-permute-done | bytes 589856 | tf_op jit(solution)/shard_map/ppermute | solution.py:410
  569.9 1.7 collective-permute-start.50
  572.2 10.2 %collective-permute-done.54 = bf16[2,384,384]{2,1,0:T(8,128)(2,1)S(1)} collective-permute-done((bf16[2,384,384]{2,1,0:T(8,128)(2,1)S(1)}, bf16[2,384,384]{2,1,0:T(8,128)(2,1)S(1)}, u32[]{:S(2)}, u32[]{:S(2)}) %collective-permute-start.54) | collective-permute-done | bytes 589856 | tf_op jit(solution)/shard_map/ppermute | solution.py:410
  582.6 1.7 collective-permute-start.55
  584.8 5.5 collective-permute-done.50
  591.4 2.4 collective-permute-done.55
  595.0 24.5 %attend_back.1 = (bf16[192,1536]{1,0:T(8,128)(2,1)}, bf16[192,1536]{1,0:T(8,128)(2,1)}, bf16[192,1536]{1,0:T(8,128)(2,1)}) custom-call(bf16[192,1536]{1,0:T(8,128)(2,1)} %get-tuple-element.54.q_ref, bf16[192,1536]{1,0:T(8,128)(2,1)} %slice.244.k_ref, bf16[192,1536]{1,0:T(8,128)(2,1)} %get-tuple-element.53.v_ref, bf16[192,1536]{1,0:T(8,128)(2,1)} %bitcast.228, ...), custom_call_target="tpu_custom_call" | custom-call | flops 18119393280 | bytes 28311552 | tf_op jit(solution)/shard_map/attend_back/pallas_call | solution.py:385
  621.9 3.5 convolution_convert_fusion.2
  625.4 4.1 fusion.21
  634.5 41.2 %psum.31 = f32[8,1152]{1,0:T(8,128)S(1)} all-reduce(f32[8,1152]{1,0:T(8,128)S(1)} %concatenate.27), channel_id=1, replica_groups=mesh['shard'=8,'ctx'=4] {'shard','ctx'}, use_global_device_ids=true, to_apply=%region_21.22 | all-reduce | flops 9216 | bytes 73728 | tf_op jit(solution)/shard_map/psum | solution.py:612
  678.4 2.3 collective-permute-start.39
  681.5 2.5 collective-permute-done.39
  684.1 1.8 collective-permute-start.40
  688.6 2.2 collective-permute-done.38
  691.2 28.7 %all_gather.15 = bf16[96,3,768]{0,1,2:T(4,128)(2,1)S(1)} all-gather(bf16[96,3,192]{0,1,2:T(4,128)(2,1)S(1)} %copy.81), channel_id=1, replica_groups=mesh['shard'=8,'ctx'=4] {'ctx'}, dimensions={2}, use_global_device_ids=true | all-gather | bytes 552960 | tf_op jit(solution)/shard_map/all_gather | solution.py:601
  723.2 2.2 convert_element_type.573
  726.5 2.3 add_bitcast_fusion
  (355 shorter events, 77.5 us)
Async XLA Ops:
  7.2 92.8 %all-gather.5.cloned.1.call-start = ((), (), s32[]{:S(2)}) async-start(), calls=%async_computation.4 | async-start | bytes 2949120 | tf_op jit(solution)/shard_map/all_gather | solution.py:533
  10.4 6.3 collective-permute-start
  14.9 6.4 collective-permute-start.4
  14.9 8.9 %collective-permute-start.9 = (bf16[96,768]{1,0:T(8,128)(2,1)S(1)}, bf16[96,768]{1,0:T(8,128)(2,1)S(1)}, u32[]{:S(2)}, u32[]{:S(2)}) collective-permute-start(bf16[96,768]{1,0:T(8,128)(2,1)S(1)} %copy-done.25), channel_id=1, source_target_pairs={{0,8},{4,12},{8,0},{12,4},{16,24},{20,28},{24,16},{28,20},{1,9},{5... | collective-permute-start | bytes 442376 | tf_op jit(solution)/shard_map/ppermute | solution.py:410
  15.5 8.6 %collective-permute-start.10 = (bf16[96,768]{1,0:T(8,128)(2,1)S(1)}, bf16[96,768]{1,0:T(8,128)(2,1)S(1)}, u32[]{:S(2)}, u32[]{:S(2)}) collective-permute-start(bf16[96,768]{1,0:T(8,128)(2,1)S(1)} %copy-done.25), channel_id=1, source_target_pairs={{0,16},{4,20},{8,24},{12,28},{16,0},{20,4},{24,8},{28,12},{1,17},{... | collective-permute-start | bytes 442376 | tf_op jit(solution)/shard_map/ppermute | solution.py:410
  16.7 9.1 %collective-permute-start.2 = (bf16[48,576]{1,0:T(8,128)(2,1)S(1)}, bf16[48,576]{1,0:T(8,128)(2,1)S(1)}, u32[]{:S(2)}, u32[]{:S(2)}) collective-permute-start(bf16[48,576]{1,0:T(8,128)(2,1)S(1)} %slice.200), channel_id=1, source_target_pairs={{0,16},{4,20},{8,24},{12,28},{16,0},{20,4},{24,8},{28,12},{1,17},{... | collective-permute-start | bytes 165896 | tf_op jit(solution)/shard_map/ppermute | solution.py:410
  18.7 7.3 collective-permute-start.3
  21.3 6.7 collective-permute-start.5
  23.9 70.6 %collective-permute-start.18 = (bf16[96,3072]{1,0:T(8,128)(2,1)}, bf16[96,3072]{1,0:T(8,128)(2,1)S(1)}, u32[]{:S(2)}, u32[]{:S(2)}) collective-permute-start(bf16[96,3072]{1,0:T(8,128)(2,1)} %refs_0_.4), channel_id=1, source_target_pairs={{0,8},{4,12},{8,0},{12,4},{16,24},{20,28},{24,16},{28,20},{1,9},{5... | collective-permute-start | bytes 1769480 | tf_op jit(solution)/shard_map/ppermute | solution.py:410
  24.0 71.6 %collective-permute-start.19 = (bf16[96,3072]{1,0:T(8,128)(2,1)}, bf16[96,3072]{1,0:T(8,128)(2,1)S(1)}, u32[]{:S(2)}, u32[]{:S(2)}) collective-permute-start(bf16[96,3072]{1,0:T(8,128)(2,1)} %refs_0_.4), channel_id=1, source_target_pairs={{0,16},{4,20},{8,24},{12,28},{16,0},{20,4},{24,8},{28,12},{1,17},{... | collective-permute-start | bytes 1769480 | tf_op jit(solution)/shard_map/ppermute | solution.py:410
  25.8 70.9 %collective-permute-start.27 = (bf16[384,768]{1,0:T(8,128)(2,1)}, bf16[384,768]{1,0:T(8,128)(2,1)S(1)}, u32[]{:S(2)}, u32[]{:S(2)}) collective-permute-start(bf16[384,768]{1,0:T(8,128)(2,1)} %refs_0_.5), channel_id=1, source_target_pairs={{0,8},{4,12},{8,0},{12,4},{16,24},{20,28},{24,16},{28,20},{1,9},{5... | collective-permute-start | bytes 1769480 | tf_op jit(solution)/shard_map/ppermute | solution.py:410
  26.1 73.0 %collective-permute-start.28 = (bf16[384,768]{1,0:T(8,128)(2,1)}, bf16[384,768]{1,0:T(8,128)(2,1)S(1)}, u32[]{:S(2)}, u32[]{:S(2)}) collective-permute-start(bf16[384,768]{1,0:T(8,128)(2,1)} %refs_0_.5), channel_id=1, source_target_pairs={{0,16},{4,20},{8,24},{12,28},{16,0},{20,4},{24,8},{28,12},{1,17},{... | collective-permute-start | bytes 1769480 | tf_op jit(solution)/shard_map/ppermute | solution.py:410
  28.0 29.0 %collective-permute-start.6 = (bf16[96,576]{1,0:T(8,128)(2,1)S(1)}, bf16[96,576]{1,0:T(8,128)(2,1)S(1)}, u32[]{:S(2)}, u32[]{:S(2)}) collective-permute-start(bf16[96,576]{1,0:T(8,128)(2,1)S(1)} %collective-permute-done.1.refs_2_), channel_id=1, source_target_pairs={{0,4},{4,0},{8,12},{12,8},{16,20},{20,16},{24,28},{28,24},{1,5},{5... | collective-permute-start | bytes 331784 | tf_op jit(solution)/shard_map/ppermute | solution.py:410
  63.3 47.6 %collective-permute-start.22 = (bf16[96,3072]{1,0:T(8,128)(2,1)}, bf16[96,3072]{1,0:T(8,128)(2,1)}, u32[]{:S(2)}, u32[]{:S(2)}) collective-permute-start(bf16[96,3072]{1,0:T(8,128)(2,1)} %refs_0_.4), channel_id=1, source_target_pairs={{0,4},{4,0},{8,12},{12,8},{16,20},{20,16},{24,28},{28,24},{1,5},{5... | collective-permute-start | bytes 1769480 | tf_op jit(solution)/shard_map/ppermute | solution.py:410
  94.5 9.1 %collective-permute-start.13 = (bf16[96,768]{1,0:T(8,128)(2,1)}, bf16[96,768]{1,0:T(8,128)(2,1)}, u32[]{:S(2)}, u32[]{:S(2)}) collective-permute-start(bf16[96,768]{1,0:T(8,128)(2,1)} %refs_0_.3), channel_id=1, source_target_pairs={{0,4},{4,0},{8,12},{12,8},{16,20},{20,16},{24,28},{28,24},{1,5},{5... | collective-permute-start | bytes 442376 | tf_op jit(solution)/shard_map/ppermute | solution.py:410
  95.7 8.4 %collective-permute-start.11 = (bf16[48,768]{1,0:T(8,128)(2,1)}, bf16[48,768]{1,0:T(8,128)(2,1)}, u32[]{:S(2)}, u32[]{:S(2)}) collective-permute-start(bf16[48,768]{1,0:T(8,128)(2,1)} %slice.207), channel_id=1, source_target_pairs={{0,16},{4,20},{8,24},{12,28},{16,0},{20,4},{24,8},{28,12},{1,17},{... | collective-permute-start | bytes 221192 | tf_op jit(solution)/shard_map/ppermute | solution.py:410
  96.7 7.5 %collective-permute-start.12 = (bf16[48,768]{1,0:T(8,128)(2,1)}, bf16[48,768]{1,0:T(8,128)(2,1)}, u32[]{:S(2)}, u32[]{:S(2)}) collective-permute-start(bf16[48,768]{1,0:T(8,128)(2,1)} %slice.208), channel_id=1, source_target_pairs={{0,8},{4,12},{8,0},{12,4},{16,24},{20,28},{24,16},{28,20},{1,9},{5... | collective-permute-start | bytes 221192 | tf_op jit(solution)/shard_map/ppermute | solution.py:410
  104.6 9.8 %collective-permute-start.20 = (bf16[48,3072]{1,0:T(8,128)(2,1)S(1)}, bf16[48,3072]{1,0:T(8,128)(2,1)S(1)}, u32[]{:S(2)}, u32[]{:S(2)}) collective-permute-start(bf16[48,3072]{1,0:T(8,128)(2,1)S(1)} %copy-done.22), channel_id=1, source_target_pairs={{0,16},{4,20},{8,24},{12,28},{16,0},{20,4},{24,8},{28,12},{1,17},{... | collective-permute-start | bytes 884744 | tf_op jit(solution)/shard_map/ppermute | solution.py:410
  107.3 39.9 %collective-permute-start.21 = (bf16[48,3072]{1,0:T(8,128)(2,1)}, bf16[48,3072]{1,0:T(8,128)(2,1)}, u32[]{:S(2)}, u32[]{:S(2)}) collective-permute-start(bf16[48,3072]{1,0:T(8,128)(2,1)} %slice.213), channel_id=1, source_target_pairs={{0,8},{4,12},{8,0},{12,4},{16,24},{20,28},{24,16},{28,20},{1,9},{5... | collective-permute-start | bytes 884744 | tf_op jit(solution)/shard_map/ppermute | solution.py:410
  108.9 38.3 %collective-permute-start.29 = (bf16[192,768]{1,0:T(8,128)(2,1)}, bf16[192,768]{1,0:T(8,128)(2,1)}, u32[]{:S(2)}, u32[]{:S(2)}) collective-permute-start(bf16[192,768]{1,0:T(8,128)(2,1)} %slice.215), channel_id=1, source_target_pairs={{0,16},{4,20},{8,24},{12,28},{16,0},{20,4},{24,8},{28,12},{1,17},{... | collective-permute-start | bytes 884744 | tf_op jit(solution)/shard_map/ppermute | solution.py:410
  109.2 38.5 %collective-permute-start.30 = (bf16[192,768]{1,0:T(8,128)(2,1)}, bf16[192,768]{1,0:T(8,128)(2,1)}, u32[]{:S(2)}, u32[]{:S(2)}) collective-permute-start(bf16[192,768]{1,0:T(8,128)(2,1)} %slice.216), channel_id=1, source_target_pairs={{0,8},{4,12},{8,0},{12,4},{16,24},{20,28},{24,16},{28,20},{1,9},{5... | collective-permute-start | bytes 884744 | tf_op jit(solution)/shard_map/ppermute | solution.py:410
  110.8 37.0 %collective-permute-start.23 = (bf16[96,3072]{1,0:T(8,128)(2,1)S(1)}, bf16[96,3072]{1,0:T(8,128)(2,1)S(1)}, u32[]{:S(2)}, u32[]{:S(2)}) collective-permute-start(bf16[96,3072]{1,0:T(8,128)(2,1)S(1)} %collective-permute-done.18.refs_1_), channel_id=1, source_target_pairs={{0,4},{4,0},{8,12},{12,8},{16,20},{20,16},{24,28},{28,24},{1,5},{5... | collective-permute-start | bytes 1769480 | tf_op jit(solution)/shard_map/ppermute | solution.py:410
  114.5 33.8 %collective-permute-start.24 = (bf16[96,3072]{1,0:T(8,128)(2,1)S(1)}, bf16[96,3072]{1,0:T(8,128)(2,1)}, u32[]{:S(2)}, u32[]{:S(2)}) collective-permute-start(bf16[96,3072]{1,0:T(8,128)(2,1)S(1)} %collective-permute-done.19.refs_2_), channel_id=1, source_target_pairs={{0,4},{4,0},{8,12},{12,8},{16,20},{20,16},{24,28},{28,24},{1,5},{5... | collective-permute-start | bytes 1769480 | tf_op jit(solution)/shard_map/ppermute | solution.py:410
  142.2 340.6 %all-to-all-start = ((bf16[192,4,384]{2,0,1:T(8,128)(2,1)}), bf16[192,4,384]{2,0,1:T(8,128)(2,1)S(1)}, u32[]{:S(2)}, u32[]{:S(2)}) async-start(bf16[192,4,384]{2,0,1:T(8,128)(2,1)} %bitcast.203), calls=%async_computation | async-start | bytes 1179648 | tf_op jit(solution)/shard_map/all_to_all | solution.py:558
  147.1 191.5 %collective-permute-start.31 = (bf16[384,768]{1,0:T(8,128)(2,1)}, bf16[384,768]{1,0:T(8,128)(2,1)}, u32[]{:S(2)}, u32[]{:S(2)}) collective-permute-start(bf16[384,768]{1,0:T(8,128)(2,1)} %refs_0_.5), channel_id=1, source_target_pairs={{0,4},{4,0},{8,12},{12,8},{16,20},{20,16},{24,28},{28,24},{1,5},{5... | collective-permute-start | bytes 1769480 | tf_op jit(solution)/shard_map/ppermute | solution.py:410
  147.2 191.4 %collective-permute-start.32 = (bf16[384,768]{1,0:T(8,128)(2,1)S(1)}, bf16[384,768]{1,0:T(8,128)(2,1)}, u32[]{:S(2)}, u32[]{:S(2)}) collective-permute-start(bf16[384,768]{1,0:T(8,128)(2,1)S(1)} %collective-permute-done.27.refs_1_), channel_id=1, source_target_pairs={{0,4},{4,0},{8,12},{12,8},{16,20},{20,16},{24,28},{28,24},{1,5},{5... | collective-permute-start | bytes 1769480 | tf_op jit(solution)/shard_map/ppermute | solution.py:410
  147.7 190.9 %collective-permute-start.33 = (bf16[384,768]{1,0:T(8,128)(2,1)S(1)}, bf16[384,768]{1,0:T(8,128)(2,1)}, u32[]{:S(2)}, u32[]{:S(2)}) collective-permute-start(bf16[384,768]{1,0:T(8,128)(2,1)S(1)} %collective-permute-done.28.refs_2_), channel_id=1, source_target_pairs={{0,4},{4,0},{8,12},{12,8},{16,20},{20,16},{24,28},{28,24},{1,5},{5... | collective-permute-start | bytes 1769480 | tf_op jit(solution)/shard_map/ppermute | solution.py:410
  150.7 187.9 %collective-permute-start.34 = (bf16[192,768]{1,0:T(8,128)(2,1)}, bf16[192,768]{1,0:T(8,128)(2,1)}, u32[]{:S(2)}, u32[]{:S(2)}) collective-permute-start(bf16[192,768]{1,0:T(8,128)(2,1)} %collective-permute-done.29.refs_3_), channel_id=1, source_target_pairs={{0,4},{4,0},{8,12},{12,8},{16,20},{20,16},{24,28},{28,24},{1,5},{5... | collective-permute-start | bytes 884744 | tf_op jit(solution)/shard_map/ppermute | solution.py:410
  151.6 187.1 %collective-permute-start.35 = (bf16[192,768]{1,0:T(8,128)(2,1)}, bf16[192,768]{1,0:T(8,128)(2,1)}, u32[]{:S(2)}, u32[]{:S(2)}) collective-permute-start(bf16[192,768]{1,0:T(8,128)(2,1)} %collective-permute-done.30.refs_4_), channel_id=1, source_target_pairs={{0,4},{4,0},{8,12},{12,8},{16,20},{20,16},{24,28},{28,24},{1,5},{5... | collective-permute-start | bytes 884744 | tf_op jit(solution)/shard_map/ppermute | solution.py:410
  523.9 7.4 %collective-permute-start.41 = (bf16[4,96,768]{2,1,0:T(8,128)(2,1)}, bf16[4,96,768]{2,1,0:T(8,128)(2,1)}, u32[]{:S(2)}, u32[]{:S(2)}) collective-permute-start(bf16[4,96,768]{2,1,0:T(8,128)(2,1)} %dynamic-slice_bitcast_fusion.6), channel_id=1, source_target_pairs={{0,4},{4,0},{8,12},{12,8},{16,20},{20,16},{24,28},{28,24},{1,5},{5... | collective-permute-start | bytes 1769480 | tf_op jit(solution)/shard_map/ppermute | solution.py:410
  525.6 23.6 %collective-permute-start.46 = (bf16[4,96,3072]{2,1,0:T(8,128)(2,1)}, bf16[4,96,3072]{2,1,0:T(8,128)(2,1)}, u32[]{:S(2)}, u32[]{:S(2)}) collective-permute-start(bf16[4,96,3072]{2,1,0:T(8,128)(2,1)} %dynamic-slice_bitcast_fusion.1), channel_id=1, source_target_pairs={{0,4},{4,0},{8,12},{12,8},{16,20},{20,16},{24,28},{28,24},{1,5},{5... | collective-permute-start | bytes 7077896 | tf_op jit(solution)/shard_map/ppermute | solution.py:410
  525.9 22.4 %all-to-all-start.1 = ((bf16[4,192,384]{2,1,0:T(8,128)(2,1)}), bf16[4,192,384]{2,1,0:T(8,128)(2,1)S(1)}, u32[]{:S(2)}, u32[]{:S(2)}) async-start(bf16[4,192,384]{2,1,0:T(8,128)(2,1)} %bitcast.227), calls=%async_computation.1 | async-start | bytes 1179648 | tf_op jit(solution)/shard_map/all_to_all | solution.py:588
  531.1 190.5 %all-reduce.3.cloned.1.call-start = ((), (), s32[]{:S(2)}) async-start(), calls=%async_computation.5 | async-start | bytes 2654208 | tf_op jit(solution)/shard_map/psum | solution.py:617
  532.6 5.7 collective-permute-start.44
  536.4 19.1 %collective-permute-start.51 = (bf16[4,384,768]{2,1,0:T(8,128)(2,1)}, bf16[4,384,768]{2,1,0:T(8,128)(2,1)}, u32[]{:S(2)}, u32[]{:S(2)}) collective-permute-start(bf16[4,384,768]{2,1,0:T(8,128)(2,1)} %dynamic-slice_bitcast_fusion), channel_id=1, source_target_pairs={{0,4},{4,0},{8,12},{12,8},{16,20},{20,16},{24,28},{28,24},{1,5},{5... | collective-permute-start | bytes 7077896 | tf_op jit(solution)/shard_map/ppermute | solution.py:410
  536.4 6.7 collective-permute-start.42
  538.4 6.4 collective-permute-start.45
  553.4 16.3 %collective-permute-start.49 = (bf16[2,96,1536]{2,1,0:T(8,128)(2,1)S(1)}, bf16[2,96,1536]{2,1,0:T(8,128)(2,1)S(1)}, u32[]{:S(2)}, u32[]{:S(2)}) collective-permute-start(bf16[2,96,1536]{2,1,0:T(8,128)(2,1)S(1)} %dynamic-slice_bitcast_fusion.4), channel_id=1, source_target_pairs={{0,16},{4,20},{8,24},{12,28},{16,0},{20,4},{24,8},{28,12},{1,17},{... | collective-permute-start | bytes 1769480 | tf_op jit(solution)/shard_map/ppermute | solution.py:410
  555.0 16.6 %collective-permute-start.47 = (bf16[2,96,1536]{2,1,0:T(8,128)(2,1)S(1)}, bf16[2,96,1536]{2,1,0:T(8,128)(2,1)S(1)}, u32[]{:S(2)}, u32[]{:S(2)}) collective-permute-start(bf16[2,96,1536]{2,1,0:T(8,128)(2,1)S(1)} %dynamic-slice_bitcast_fusion.5), channel_id=1, source_target_pairs={{0,8},{4,12},{8,0},{12,4},{16,24},{20,28},{24,16},{28,20},{1,9},{5... | collective-permute-start | bytes 1769480 | tf_op jit(solution)/shard_map/ppermute | solution.py:410
  558.1 24.3 %collective-permute-start.54 = (bf16[2,384,384]{2,1,0:T(8,128)(2,1)S(1)}, bf16[2,384,384]{2,1,0:T(8,128)(2,1)S(1)}, u32[]{:S(2)}, u32[]{:S(2)}) collective-permute-start(bf16[2,384,384]{2,1,0:T(8,128)(2,1)S(1)} %dynamic-slice_bitcast_fusion.2), channel_id=1, source_target_pairs={{0,16},{4,20},{8,24},{12,28},{16,0},{20,4},{24,8},{28,12},{1,17},{... | collective-permute-start | bytes 1769480 | tf_op jit(solution)/shard_map/ppermute | solution.py:410
  560.0 24.3 %collective-permute-start.52 = (bf16[2,384,384]{2,1,0:T(8,128)(2,1)S(1)}, bf16[2,384,384]{2,1,0:T(8,128)(2,1)S(1)}, u32[]{:S(2)}, u32[]{:S(2)}) collective-permute-start(bf16[2,384,384]{2,1,0:T(8,128)(2,1)S(1)} %dynamic-slice_bitcast_fusion.3), channel_id=1, source_target_pairs={{0,8},{4,12},{8,0},{12,4},{16,24},{20,28},{24,16},{28,20},{1,9},{5... | collective-permute-start | bytes 1769480 | tf_op jit(solution)/shard_map/ppermute | solution.py:410
  569.9 20.4 %collective-permute-start.50 = (bf16[96,1536]{1,0:T(8,128)(2,1)S(1)}, bf16[96,1536]{1,0:T(8,128)(2,1)S(1)}, u32[]{:S(2)}, u32[]{:S(2)}) collective-permute-start(bf16[96,1536]{1,0:T(8,128)(2,1)S(1)} %dynamic-slice_bitcast_fusion.10), channel_id=1, source_target_pairs={{0,8},{4,12},{8,0},{12,4},{16,24},{20,28},{24,16},{28,20},{1,9},{5... | collective-permute-start | bytes 884744 | tf_op jit(solution)/shard_map/ppermute | solution.py:410
  571.8 18.6 %collective-permute-start.48 = (bf16[96,1536]{1,0:T(8,128)(2,1)S(1)}, bf16[96,1536]{1,0:T(8,128)(2,1)S(1)}, u32[]{:S(2)}, u32[]{:S(2)}) collective-permute-start(bf16[96,1536]{1,0:T(8,128)(2,1)S(1)} %dynamic-slice_bitcast_fusion.11), channel_id=1, source_target_pairs={{0,16},{4,20},{8,24},{12,28},{16,0},{20,4},{24,8},{28,12},{1,17},{... | collective-permute-start | bytes 884744 | tf_op jit(solution)/shard_map/ppermute | solution.py:410
  582.6 11.2 %collective-permute-start.55 = (bf16[384,384]{1,0:T(8,128)(2,1)S(1)}, bf16[384,384]{1,0:T(8,128)(2,1)S(1)}, u32[]{:S(2)}, u32[]{:S(2)}) collective-permute-start(bf16[384,384]{1,0:T(8,128)(2,1)S(1)} %dynamic-slice_bitcast_fusion.8), channel_id=1, source_target_pairs={{0,8},{4,12},{8,0},{12,4},{16,24},{20,28},{24,16},{28,20},{1,9},{5... | collective-permute-start | bytes 884744 | tf_op jit(solution)/shard_map/ppermute | solution.py:410
  584.5 9.4 %collective-permute-start.53 = (bf16[384,384]{1,0:T(8,128)(2,1)S(1)}, bf16[384,384]{1,0:T(8,128)(2,1)S(1)}, u32[]{:S(2)}, u32[]{:S(2)}) collective-permute-start(bf16[384,384]{1,0:T(8,128)(2,1)S(1)} %dynamic-slice_bitcast_fusion.9), channel_id=1, source_target_pairs={{0,16},{4,20},{8,24},{12,28},{16,0},{20,4},{24,8},{28,12},{1,17},{... | collective-permute-start | bytes 884744 | tf_op jit(solution)/shard_map/ppermute | solution.py:410
  594.9 131.6 %reduce-scatter.2.cloned.1.call-start = ((), (), s32[]{:S(2)}) async-start(), calls=%async_computation.3 | async-start | bytes 2949120 | tf_op jit(solution)/shard_map/reduce_scatter | solution.py:595
  631.9 45.1 %collective-permute-start.36 = (bf16[4,96,576]{2,1,0:T(8,128)(2,1)}, bf16[4,96,576]{2,1,0:T(8,128)(2,1)}, u32[]{:S(2)}, u32[]{:S(2)}) collective-permute-start(bf16[4,96,576]{2,1,0:T(8,128)(2,1)} %dynamic-slice_bitcast_fusion.7), channel_id=1, source_target_pairs={{0,4},{4,0},{8,12},{12,8},{16,20},{20,16},{24,28},{28,24},{1,5},{5... | collective-permute-start | bytes 1327112 | tf_op jit(solution)/shard_map/ppermute | solution.py:410
  678.4 5.7 collective-permute-start.39
  (76 other events, 1827.3 us)
Sparse Core Ops, SparseCore 0:
  9.6 53.1 all-gather.4
  595.0 62.8 all-reduce.2
  660.3 58.4 reduce-scatter.1
